TPU v7x, 32 devices: a whole 2x2x4 slice. The times are simulated.
32 devices in a mesh: tile: 8 (over z, y), visit: 4 (over x, core).
Axes of the slice: x: 2, y: 2, z: 4, core: 2. Of those that a mesh axis runs over, the one named last changes fastest.
Arguments:
- template: float32 [1024, 2048], P('tile', 'visit'), may hold values from -6 to 6
- row_taps: float32 [16, 21], replicated, may hold values from -1 to 1
- col_taps: float32 [16, 21], replicated, may hold values from -1 to 1
- coeffs: float32 [4, 16, 6], P('visit'), may hold values from -2 to 2
- visits: float32 [4, 1024, 2048], P('visit', 'tile'), may hold values from -6 to 6
- boxes: int32 [4, 2], replicated, may hold values from 0 to 2048, as said below
Outputs:
- difference: float32 [4, 1024, 2048], P('visit', 'tile')
Inputs may be any that keep to these rules, and one draw needn't show every extreme that they name: boxes[v, 0] is the first column and boxes[v, 1] the number of columns of visit v's box, which lies within the 2048 columns; boxes[v, 1] is at least 512, and some visit covers all 2048 columns.
All inputs are finite; a program needn't handle non-finite values.
Results may differ from a plain program's by a relative error of at most 0.0003.
Values sent between devices are 32-bit elements; how exact they have to be, the bound alone decides.
A program may use at most 128 MiB of HBM per device.

v0:
```python
import jax
import jax.numpy as jnp
from jax import lax
from jax.sharding import PartitionSpec as P


def extended_2(cells, sides, width):
    for axis, dim in sides:
        count = lax.axis_size(axis)
        ends = count - 1
        head = lax.slice_in_dim(cells, 0, width, axis=dim)
        tail = lax.slice_in_dim(cells, cells.shape[dim] - width, cells.shape[dim], axis=dim)
        cells = jnp.concatenate(
            [
                lax.ppermute(tail, axis, [(i, (i + 1) % count) for i in range(ends)]),
                cells,
                lax.ppermute(head, axis, [((i + 1) % count, i) for i in range(ends)]),
            ],
            axis=dim,
        )
    return cells


def coordinate(first, count, total):
    return 2.0 * ((first + jnp.arange(count)).astype(jnp.float32) + 0.5) / total - 1.0


def surface_terms(y_coord, x_coord):
    y_grid = y_coord[:, None] * jnp.ones_like(x_coord)[None, :]
    x_grid = jnp.ones_like(y_coord)[:, None] * x_coord[None, :]
    return jnp.stack(
        [jnp.ones_like(x_grid), x_grid, y_grid, x_grid * x_grid, x_grid * y_grid, y_grid * y_grid]
    )


def separable(padded, row_taps, col_taps, tile_rows, span):
    passed = jnp.zeros((row_taps.shape[0], tile_rows, padded.shape[1]), jnp.float32)
    for offset in range(row_taps.shape[1]):
        passed = (
            passed + row_taps[:, offset, None, None] * padded[None, offset : offset + tile_rows, :]
        )
    images = jnp.zeros((row_taps.shape[0], tile_rows, span), jnp.float32)
    for offset in range(col_taps.shape[1]):
        images = images + col_taps[:, offset, None, None] * passed[:, :, offset : offset + span]
    return images


def combine(coef, images, y_coord, first_col, full_width):
    terms = surface_terms(y_coord, coordinate(first_col, images.shape[2], full_width))
    weighted = jnp.einsum("vkt,krc->vtrc", coef, images, precision=lax.Precision.HIGHEST)
    return jnp.sum(weighted * terms[None], axis=1)


def local(template, row_taps, col_taps, coeffs, visits, boxes):
    half = row_taps.shape[1] // 2
    tile_rows, columns = template.shape
    full_width = columns * lax.axis_size("visit")
    total_rows = tile_rows * lax.axis_size("tile")
    y_coord = coordinate(lax.axis_index("tile") * tile_rows, tile_rows, total_rows)
    visit_count = visits.shape[0]
    extended = extended_2(template, (("tile", 0), ("visit", 1)), half)
    basis = separable(extended, row_taps, col_taps, tile_rows, columns)
    model = combine(
        coeffs,
        lax.all_gather(basis, "visit", axis=2, tiled=True),
        y_coord,
        jnp.int32(0),
        full_width,
    )
    local_boxes = lax.dynamic_slice_in_dim(
        boxes, lax.axis_index("visit") * visit_count, visit_count, 0
    )
    column_index = jnp.arange(full_width)
    inside = (column_index[None, :] >= local_boxes[:, 0:1]) & (
        column_index[None, :] < local_boxes[:, 0:1] + local_boxes[:, 1:2]
    )
    return jnp.where(inside[:, None, :], visits - model, jnp.float32(0.0))


def solution(mesh):
    placed = (P("tile", "visit"), P(), P(), P("visit", None, None), P("visit", "tile", None), P())
    return jax.shard_map(
        local, mesh=mesh, in_specs=placed, out_specs=P("visit", "tile", None), check_vma=False
    )
```

profile of v0, /device:TPU:0, one launch (start us, length us, event | category | flops | bytes accessed | tf_op | source)
XLA Modules:
  0.0 223.0 jit_solution(3246250669561750262)
XLA Ops:
  6.5 0.8 fusion.29
  7.3 1.3 collective-permute-start.1
  8.6 5.5 %collective-permute-start = (f32[10,512]{1,0:T(8,128)S(1)}, f32[10,512]{1,0:T(8,128)S(1)}, u32[]{:S(2)}, u32[]{:S(2)}) collective-permute-start(f32[10,512]{1,0:T(8,128)S(1)} %get-tuple-element.70), channel_id=1, source_target_pairs={{0,4},{4,8},{8,12},{12,16},{16,20},{20,24},{24,28},{1,5},{5,9},{9,... | collective-permute-start | bytes 61448 | tf_op jit(solution)/shard_map/ppermute | solution.py:15
  14.1 2.5 %slice_reduce_fusion.40 = (f32[16]{0:T(128)S(1)}, f32[16]{0:T(128)S(1)}, f32[16]{0:T(128)S(1)}, f32[16]{0:T(128)S(1)}, f32[16]{0:T(128)S(1)}, /*index=5*/f32[16]...) fusion(f32[16,21]{1,0:T(8,128)} %param.7), kind=kLoop, calls=%fused_computation.92 | loop fusion | bytes 2432 | tf_op jit(solution)/shard_map/slice | solution.py:40
  16.6 1.9 slice_reduce_fusion.41
  18.6 1.0 slice_reduce_fusion.21
  19.5 0.0 collective-permute-done.1
  19.5 0.0 collective-permute-done
  19.6 1.0 pad_maximum_fusion.3
  20.5 1.3 collective-permute-start.3
  21.8 3.0 %collective-permute-start.2 = (f32[148,10]{1,0:T(8,128)S(1)}, f32[148,10]{1,0:T(8,128)S(1)}, u32[]{:S(2)}, u32[]{:S(2)}) collective-permute-start(f32[148,10]{1,0:T(8,128)S(1)} %get-tuple-element.68), channel_id=1, source_target_pairs={{0,1},{1,2},{2,3},{4,5},{5,6},{6,7},{8,9},{9,10},{10,11},{12,13},{... | collective-permute-start | bytes 17768 | tf_op jit(solution)/shard_map/ppermute | solution.py:15
  24.9 1.0 slice_reduce_fusion.1
  25.8 0.0 collective-permute-done.2
  25.8 1.2 pad_maximum_fusion
  27.0 0.5 fusion.27
  27.5 8.8 %multiply_add_fusion = f32[16,128,532]{2,0,1:T(8,128)} fusion(f32[128,532]{1,0:T(8,128)S(1)} %get-tuple-element.48, f32[16]{0:T(128)S(1)} %get-tuple-element.46, f32[128,532]{1,0:T(8,128)S(1)} %get-tuple-element.49, f32[16]{0:T(128)S(1)} %get-tuple-element.45, f32[128,532]{1,0:T(8,128)S(1)} %get-tuple-element.50, f32[16]{0:T(128)S(1)} %get-tuple-element.27, ...), kind=kLoop, calls=%fused_computation.2 | loop fusion | flops 44670976 | bytes 10079552 | tf_op jit(solution)/shard_map/add | solution.py:40
  36.4 51.5 %fusion.1 = f32[16,128,512]{2,0,1:T(8,128)} fusion(f32[16,128,532]{2,0,1:T(8,128)} %multiply_add_fusion, f32[16]{0:T(128)S(1)} %get-tuple-element.25, f32[16]{0:T(128)S(1)} %get-tuple-element.24, f32[16]{0:T(128)S(1)} %get-tuple-element.6, f32[16]{0:T(128)S(1)} %get-tuple-element.7, f32[16]{0:T(128)S(1)} %get-tuple-element.8, f32[16]{0:T(128)S(1)} %get-tuple-element.9, ...), kind=kLoop, calls=%fused_computation.4 | loop fusion | flops 42991616 | bytes 92276032 | tf_op jit(solution)/shard_map/add | solution.py:44
  87.8 0.0 all-gather.2.cloned.1.call-update
  87.9 0.1 constant_dynamic-slice_fusion
  88.0 0.6 fusion.30
  89.9 0.6 broadcast_multiply_fusion
  90.6 0.5 stack.18
  91.1 0.6 stack.19
  91.7 1.6 stack.20
  93.3 1.6 stack.21
  94.9 1.5 stack_broadcast_in_dim.3
  96.4 20.5 %stack.22 = f32[6,128,2048]{2,0,1:T(8,128)} concatenate(f32[1,128,2048]{2,0,1:T(1,128)} %stack_broadcast_in_dim.3, f32[1,128,2048]{2,0,1:T(1,128)S(1)} %stack.18, f32[1,128,2048]{2,0,1:T(1,128)S(1)} %stack.19, f32[1,128,2048]{2,0,1:T(1,128)} %stack.20, f32[1,128,2048]{2,0,1:T(1,128)S(1)} %broadcast_multiply_fusion, f32[1,128,2048]{2,0,1:T(1,128)} %stack.21), dimensions={0} | concatenate | bytes 12582912 | tf_op jit(solution)/shard_map/stack | solution.py:31
  116.9 0.7 fusion.22
  117.6 0.0 copy-start.1
  117.6 80.3 %all-gather.2.cloned.1.call-done = f32[16,128,2048]{2,0,1:T(8,128)} async-done(((f32[16,128,512]{2,0,1:T(8,128)}), f32[16,128,2048]{2,0,1:T(8,128)}) %all-gather.2.cloned.1.call-update) | async-done | bytes 16777232 | tf_op jit(solution)/shard_map/all_gather | solution.py:65
  197.9 17.1 %fusion = f32[128,2048]{1,0:T(8,128)S(1)} fusion(f32[6,128,2048]{2,0,1:T(8,128)} %stack.22, f32[16,128,2048]{2,0,1:T(8,128)} %all-gather.2.cloned.1.call-done, f32[1,16,6]{1,0,2:T(1,128)S(1)} %copy-done.2), kind=kOutput, calls=%fused_computation.1 | convolution fusion | flops 304873472 | bytes 24117632 | tf_op jit(solution)/shard_map/vkt,krc->vtrc/dot_general | solution.py:50
  215.1 1.1 fusion.21
  (11 shorter events, 0.1 us)
Async XLA Ops:
  6.5 81.3 %copy-start = (s32[4,2]{0,1:T(2,128)S(1)}, s32[4,2]{0,1:T(2,128)}, u32[]{:S(2)}) copy-start(s32[4,2]{0,1:T(2,128)} %param.11) | copy-start | bytes 100
  6.5 191.4 %all-gather.2.cloned.1.call-start = ((), (), s32[]{:S(2)}) async-start(), calls=%async_computation | async-start | bytes 20971520 | tf_op jit(solution)/shard_map/all_gather | solution.py:65
  7.3 12.2 %collective-permute-start.1 = (f32[10,512]{1,0:T(8,128)S(1)}, f32[10,512]{1,0:T(8,128)S(1)}, u32[]{:S(2)}, u32[]{:S(2)}) collective-permute-start(f32[10,512]{1,0:T(8,128)S(1)} %get-tuple-element.71), channel_id=1, source_target_pairs={{4,0},{8,4},{12,8},{16,12},{20,16},{24,20},{28,24},{5,1},{9,5},{13... | collective-permute-start | bytes 61448 | tf_op jit(solution)/shard_map/ppermute | solution.py:17
  8.6 10.9 %collective-permute-start = (f32[10,512]{1,0:T(8,128)S(1)}, f32[10,512]{1,0:T(8,128)S(1)}, u32[]{:S(2)}, u32[]{:S(2)}) collective-permute-start(f32[10,512]{1,0:T(8,128)S(1)} %get-tuple-element.70), channel_id=1, source_target_pairs={{0,4},{4,8},{8,12},{12,16},{16,20},{20,24},{24,28},{1,5},{5,9},{9,... | collective-permute-start | bytes 61448 | tf_op jit(solution)/shard_map/ppermute | solution.py:15
  20.5 5.3 %collective-permute-start.3 = (f32[148,10]{1,0:T(8,128)S(1)}, f32[148,10]{1,0:T(8,128)S(1)}, u32[]{:S(2)}, u32[]{:S(2)}) collective-permute-start(f32[148,10]{1,0:T(8,128)S(1)} %get-tuple-element.69), channel_id=1, source_target_pairs={{1,0},{2,1},{3,2},{5,4},{6,5},{7,6},{9,8},{10,9},{11,10},{13,12},{... | collective-permute-start | bytes 17768 | tf_op jit(solution)/shard_map/ppermute | solution.py:17
  21.8 4.0 %collective-permute-start.2 = (f32[148,10]{1,0:T(8,128)S(1)}, f32[148,10]{1,0:T(8,128)S(1)}, u32[]{:S(2)}, u32[]{:S(2)}) collective-permute-start(f32[148,10]{1,0:T(8,128)S(1)} %get-tuple-element.68), channel_id=1, source_target_pairs={{0,1},{1,2},{2,3},{4,5},{5,6},{6,7},{8,9},{9,10},{10,11},{12,13},{... | collective-permute-start | bytes 17768 | tf_op jit(solution)/shard_map/ppermute | solution.py:15
  96.4 101.5 %copy-start.2 = (f32[1,16,6]{1,0,2:T(1,128)S(1)}, f32[1,16,6]{1,0,2:T(1,128)}, u32[]{:S(2)}) copy-start(f32[1,16,6]{1,0,2:T(1,128)} %param.9) | copy-start | bytes 1156
  117.6 97.5 %copy-start.1 = (f32[1,128,2048]{2,1,0:T(8,128)S(1)}, f32[1,128,2048]{2,1,0:T(8,128)}, u32[]{:S(2)}) copy-start(f32[1,128,2048]{2,1,0:T(8,128)} %param.10) | copy-start | bytes 3145732
Sparse Core Ops, SparseCore 0:
  88.0 109.8 all-gather.1
where the time goes:
time: 226 us; the launch traced here: 223 us
  waiting for transfers between devices  80.4 us (36%)
  other arithmetic  64.8 us (29%)
  local copies, waits for them, and re-layouts  34.7 us (15%)
  matrix products  17.1 us (8%)
  between operations  14.9 us (7%)
  starting transfers between devices  11.1 us (5%)
    all_gather x1, waiting for transfers between devices, local(): lax.all_gather(basis, 'visit', axis=2, tiled=True)  80.3 us
    add x1, other arithmetic, separable(): images + col_taps[:, offset, None, None] * passed[:, :, offset:offset + s...  51.5 us
    another operation x6, local copies, waits for them, and re-layouts, surface_terms(): jnp.stack([jnp.ones_like(x_grid), x_grid, y_grid, x_grid * x_grid, x_grid...  26.3 us
    dot_general x1, matrix products, combine(): jnp.einsum('vkt,krc->vtrc', coef, images, precision=lax.Precision.HIGHEST)  17.1 us
    add x1, other arithmetic, separable(): passed + row_taps[:, offset, None, None] * padded[None, offset:offset + t...  8.83 us
    ppermute x2, starting transfers between devices, extended_2(): lax.ppermute(tail, axis, [(i, (i + 1) % count) for i in range(ends)])  8.54 us
  transfers between devices with their start and end apart: 5, of which 1 were waited for; matrix products, arithmetic and copies ran while one was open for 16% of the time, Pallas kernels for 0%

commit v1 on v0

v1 whole, which is shorter than its diff:
```python
import functools

import jax
import jax.numpy as jnp
from jax import lax
from jax.experimental import pallas as pl
from jax.experimental.pallas import tpu as pltpu
from jax.sharding import PartitionSpec as P

BLOCK = 64
WINDOW = 96
LANES = 128
CHUNK = 256


def split(value):
    high = value.astype(jnp.bfloat16)
    low = (value - high.astype(jnp.float32)).astype(jnp.bfloat16)
    return high, low


def kernel(taps, rows, columns, total_rows, meta_ref, base_ref, t_ref, vis_ref, out_ref, w_ref, s_ref):
    half = taps // 2
    blocks = rows // BLOCK
    depth = s_ref.shape[2]
    step = pl.program_id(0)

    @pl.when(step == 0)
    def _():
        rolled = [
            pltpu.roll(
                jnp.broadcast_to(base_ref[t : t + 1, :], (BLOCK, depth)), 0, 1, stride=1, stride_axis=0
            )
            for t in range(6)
        ]
        for block in range(blocks):
            row = lax.broadcasted_iota(jnp.int32, (BLOCK, 1), 0) + (meta_ref[0] + block * BLOCK)
            y = 2.0 * (row.astype(jnp.float32) + 0.5) / total_rows - 1.0
            parts = (
                rolled[0] + y * (rolled[2] + y * rolled[5]),
                rolled[1] + y * rolled[4],
                rolled[3],
            )
            for i, part in enumerate(parts):
                high, low = split(part)
                w_ref[0, block, i * BLOCK : (i + 1) * BLOCK, :] = high
                w_ref[1, block, i * BLOCK : (i + 1) * BLOCK, :] = low
        pad = depth - taps * WINDOW
        if pad:
            s_ref[:, :, taps * WINDOW :, :] = jnp.zeros((2, blocks, pad, CHUNK), jnp.bfloat16)

    window = t_ref[:, pl.ds(pl.multiple_of(step * CHUNK, CHUNK), CHUNK + 2 * LANES)]
    for which, part in enumerate(split(window)):
        for b in range(taps):
            first = LANES - half + b
            shifted = part[:, first : first + CHUNK]
            for block in range(blocks):
                s_ref[which, block, b * WINDOW : (b + 1) * WINDOW, :] = shifted[
                    block * BLOCK : block * BLOCK + WINDOW
                ]
    column = lax.broadcasted_iota(jnp.int32, (1, CHUNK), 1) + step * CHUNK
    x = 2.0 * (column.astype(jnp.float32) + 0.5) / columns - 1.0
    inside = (column >= meta_ref[1]) & (column < meta_ref[2])
    for block in range(blocks):
        dot = functools.partial(jnp.dot, preferred_element_type=jnp.float32)
        total = (
            dot(w_ref[0, block], s_ref[0, block])
            + dot(w_ref[1, block], s_ref[0, block])
            + dot(w_ref[0, block], s_ref[1, block])
        )
        model = total[:BLOCK] + x * (total[BLOCK : 2 * BLOCK] + x * total[2 * BLOCK :])
        at = slice(block * BLOCK, (block + 1) * BLOCK)
        out_ref[at, :] = jnp.where(inside, vis_ref[at, :] - model, 0.0)


def bases(coeffs, row_taps, col_taps, depth):
    weight = jnp.sum(
        coeffs.T[:, :, None, None] * col_taps[None, :, :, None] * row_taps[None, :, None, :], axis=1
    )
    taps = row_taps.shape[1]
    base = jnp.pad(weight, ((0, 2), (0, 0), (0, WINDOW - taps))).reshape(8, taps * WINDOW)
    return jnp.pad(base, ((0, 0), (0, depth - taps * WINDOW)))


def local(template, row_taps, col_taps, coeffs, visits, boxes):
    taps = row_taps.shape[1]
    half = taps // 2
    rows, width = template.shape
    columns = width * lax.axis_size("visit")
    count = lax.axis_size("tile")
    blocks = rows // BLOCK
    tall = (blocks - 1) * BLOCK + WINDOW
    depth = -(-taps * WINDOW // 256) * 256
    above = lax.ppermute(template[rows - half :], "tile", [(i, i + 1) for i in range(count - 1)])
    below = lax.ppermute(template[:half], "tile", [(i + 1, i) for i in range(count - 1)])
    slab = jnp.concatenate([above, template, below], axis=0)
    slab = lax.all_gather(slab, "visit", axis=1, tiled=True)
    slab = jnp.pad(slab, ((0, tall - slab.shape[0]), (LANES, LANES)))
    base = bases(coeffs[0], row_taps, col_taps, depth)
    box = lax.dynamic_slice_in_dim(boxes, lax.axis_index("visit"), 1, 0)[0]
    meta = jnp.stack([lax.axis_index("tile").astype(jnp.int32) * rows, box[0], box[0] + box[1]])
    out = pl.pallas_call(
        functools.partial(kernel, taps, rows, columns, rows * count),
        grid=(columns // CHUNK,),
        in_specs=[
            pl.BlockSpec(memory_space=pltpu.SMEM),
            pl.BlockSpec((8, depth), lambda g: (0, 0)),
            pl.BlockSpec((tall, columns + 2 * LANES), lambda g: (0, 0)),
            pl.BlockSpec((rows, CHUNK), lambda g: (0, g)),
        ],
        out_specs=pl.BlockSpec((rows, CHUNK), lambda g: (0, g)),
        out_shape=jax.ShapeDtypeStruct((rows, columns), jnp.float32),
        scratch_shapes=[
            pltpu.VMEM((2, blocks, 3 * BLOCK, depth), jnp.bfloat16),
            pltpu.VMEM((2, blocks, depth, CHUNK), jnp.bfloat16),
        ],
        compiler_params=pltpu.CompilerParams(vmem_limit_bytes=48 * 2**20),
    )(meta, base, slab, visits[0])
    return out[None]


def solution(mesh):
    placed = (P("tile", "visit"), P(), P(), P("visit", None, None), P("visit", "tile", None), P())
    return jax.shard_map(
        local, mesh=mesh, in_specs=placed, out_specs=P("visit", "tile", None), check_vma=False
    )
```

time: 226 us -> 67 us (0.30); the launches traced: 223 us -> 66.5 us
  waiting for transfers between devices: 80.4 us -> 18.4 us
  other arithmetic: 64.8 us -> 3.45 us
  local copies, waits for them, and re-layouts: 34.7 us -> 4.43 us
  Pallas kernels: 0 us -> 19.4 us
  matrix products: 17.1 us -> 0 us
  starting transfers between devices: 11.1 us -> 6.15 us
    all_gather x1, waiting for transfers between devices: 80.3 us -> 13.9 us  [local(): slab = lax.all_gather(slab, 'visit', axis=1, tiled=True)]
    add x2 -> x0, other arithmetic: 60.3 us -> none  [the longest x1 51.5 us: separable(): images + col_taps[:, offset, None, None] * passed[:, :, offset:offset + s...]
    another operation x6 -> x0, local copies, waits for them, and re-layouts: 26.3 us -> none  [surface_terms(): jnp.stack([jnp.ones_like(x_grid), x_grid, y_grid, x_grid * x_grid, x_grid...]
    pallas_call x0 -> x1, Pallas kernels: none -> 19.4 us  [local(): pl.pallas_call(functools.partial(kernel, taps, rows, columns, rows * coun...]
    dot_general x1 -> x0, matrix products: 17.1 us -> none  [combine(): jnp.einsum('vkt,krc->vtrc', coef, images, precision=lax.Precision.HIGHEST)]
    slice x8 -> x2, local copies, waits for them, and re-layouts: 8.27 us -> 1.38 us  [the longest x1 0.79 us: local(): template[rows - half:]]
    ppermute x4 -> x2, starting transfers between devices: 11.1 us -> 6.15 us  [the longest x1 4.86 us: local(): lax.ppermute(template[rows - half:], 'tile', [(i, i + 1) for i in range(c...]
    ppermute x4 -> x2, waiting for transfers between devices: 0.01 us -> 4.51 us  [the longest x1 4.23 us: local(): lax.ppermute(template[:half], 'tile', [(i + 1, i) for i in range(count -...]
  transfers between devices with their start and end apart: 5 -> 3, of which waited for: 1 -> 3; matrix products, arithmetic and copies ran while one was open for 16% -> 6% of each run, Pallas kernels for 0% -> 0%
where the time goes in v1:
time: 67 us; the launch traced here: 66.5 us
  Pallas kernels  19.4 us (29%)
  waiting for transfers between devices  18.4 us (27%)
  between operations  14.7 us (22%)
  starting transfers between devices  6.15 us (9%)
  local copies, waits for them, and re-layouts  4.43 us (7%)
  other arithmetic  3.45 us (5%)
    pallas_call x1, Pallas kernels, local(): pl.pallas_call(functools.partial(kernel, taps, rows, columns, rows * coun...  19.4 us
    all_gather x1, waiting for transfers between devices, local(): slab = lax.all_gather(slab, 'visit', axis=1, tiled=True)  13.9 us
    ppermute x1, starting transfers between devices, local(): lax.ppermute(template[rows - half:], 'tile', [(i, i + 1) for i in range(c...  4.86 us
    ppermute x1, waiting for transfers between devices, local(): lax.ppermute(template[:half], 'tile', [(i + 1, i) for i in range(count -...  4.23 us
    concatenate x1, other arithmetic, local(): slab = jnp.concatenate([above, template, below], axis=0)  1.71 us
    unnamed x6, local copies, waits for them, and re-layouts  1.48 us
    pad x1, local copies, waits for them, and re-layouts, local(): slab = jnp.pad(slab, ((0, tall - slab.shape[0]), (LANES, LANES)))  1.39 us
  transfers between devices with their start and end apart: 3, of which 3 were waited for; matrix products, arithmetic and copies ran while one was open for 6% of the time, Pallas kernels for 0%

profile of v1, /device:TPU:0, one launch (start us, length us, event | category | flops | bytes accessed | tf_op | source)
XLA Modules:
  0.0 66.5 jit_solution(10644344827194654831)
XLA Ops:
  6.5 0.0 copy-start
  6.5 0.0 all-gather.2.cloned.1.call-start
  6.5 0.8 %fusion = (f32[10,512]{1,0:T(8,128)S(1)}, f32[10,512]{1,0:T(8,128)S(1)}) fusion(f32[128,512]{1,0:T(8,128)} %param.6), kind=kLoop, calls=%fused_computation.6 | loop fusion | bytes 81920 | tf_op jit(solution)/shard_map/slice | solution.py:94
  7.3 4.9 %collective-permute-start = (f32[10,512]{1,0:T(8,128)S(1)}, f32[10,512]{1,0:T(8,128)S(1)}, u32[]{:S(2)}, u32[]{:S(2)}) collective-permute-start(f32[10,512]{1,0:T(8,128)S(1)} %get-tuple-element.5), channel_id=1, source_target_pairs={{0,4},{4,8},{8,12},{12,16},{16,20},{20,24},{24,28},{1,5},{5,9},{9,... | collective-permute-start | bytes 61448 | tf_op jit(solution)/shard_map/ppermute | solution.py:94
  12.2 1.3 %collective-permute-start.1 = (f32[10,512]{1,0:T(8,128)S(1)}, f32[10,512]{1,0:T(8,128)S(1)}, u32[]{:S(2)}, u32[]{:S(2)}) collective-permute-start(f32[10,512]{1,0:T(8,128)S(1)} %get-tuple-element.6), channel_id=1, source_target_pairs={{4,0},{8,4},{12,8},{16,12},{20,16},{24,20},{28,24},{5,1},{9,5},{13... | collective-permute-start | bytes 61448 | tf_op jit(solution)/shard_map/ppermute | solution.py:95
  13.5 0.3 collective-permute-done
  13.8 4.2 %collective-permute-done.1 = f32[10,512]{1,0:T(8,128)S(1)} collective-permute-done((f32[10,512]{1,0:T(8,128)S(1)}, f32[10,512]{1,0:T(8,128)S(1)}, u32[]{:S(2)}, u32[]{:S(2)}) %collective-permute-start.1) | collective-permute-done | bytes 20512 | tf_op jit(solution)/shard_map/ppermute | solution.py:95
  18.0 1.7 %pad_maximum_fusion = f32[148,512]{1,0:T(8,128)} fusion(f32[10,512]{1,0:T(8,128)S(1)} %collective-permute-done.1, f32[128,512]{1,0:T(8,128)} %param.6, f32[10,512]{1,0:T(8,128)S(1)} %collective-permute-done), kind=kLoop, calls=%fused_computation.1 | loop fusion | flops 151552 | bytes 606208 | tf_op jit(solution)/shard_map/concatenate | solution.py:96
  19.7 0.0 all-gather.2.cloned.1.call-update
  19.7 0.8 %copy.7 = f32[16,21]{0,1:T(8,128)S(1)} copy(f32[16,21]{1,0:T(8,128)} %param.8) | data formatting | bytes 2688 | tf_op args[2]
  20.5 0.7 %copy.10 = f32[1,16,6]{1,2,0:T(8,128)S(1)} copy(f32[1,16,6]{1,0,2:T(1,128)} %param.9) | data formatting | bytes 768
  21.2 1.1 %multiply_reduce_fusion = f32[6,21,21]{2,1,0:T(8,128)S(1)} fusion(f32[16,21]{1,0:T(8,128)} %param.7, f32[6,16,21]{1,2,0:T(8,128)S(1)} %broadcast_multiply_fusion), kind=kLoop, calls=%fused_computation | loop fusion | flops 82026 | bytes 19992 | tf_op jit(solution)/shard_map/reduce_sum | solution.py:77
  22.3 0.1 reshape.19
  22.4 0.0 copy-start.1
  22.5 0.0 copy-done
  22.5 0.1 constant_dynamic-slice_fusion
  22.5 0.6 fusion.1
  24.3 0.6 pad_add_fusion.meta_ref
  25.0 13.9 %all-gather.2.cloned.1.call-done = f32[148,2048]{1,0:T(8,128)} async-done(((f32[148,512]{1,0:T(8,128)}), f32[148,2048]{1,0:T(8,128)}) %all-gather.2.cloned.1.call-update) | async-done | bytes 1212432 | tf_op jit(solution)/shard_map/all_gather | solution.py:97
  38.9 1.4 %pad.14.t_ref = f32[160,2304]{1,0:T(8,128)S(1)} pad(f32[148,2048]{1,0:T(8,128)} %all-gather.2.cloned.1.call-done, f32[]{:T(128)} %constant.17.clone.1), padding=0_12x128_128 | pad | bytes 2686980 | tf_op jit(solution)/shard_map/jit(_pad)/pad | solution.py:98
  40.3 0.0 copy-done.1
  40.3 19.4 %shard_map.64 = f32[128,2048]{1,0:T(8,128)} custom-call(s32[3]{0:T(128)S(1)} %pad_add_fusion.meta_ref, f32[8,2048]{1,0:T(8,128)S(1)} %pad.13.base_ref, f32[160,2304]{1,0:T(8,128)S(1)} %pad.14.t_ref, f32[128,2048]{1,0:T(8,128)S(1)} %bitcast.10), custom_call_target="tpu_custom_call" | custom-call | tf_op jit(solution)/shard_map/pallas_call | solution.py:102
  (3 shorter events, 0.0 us)
Async XLA Ops:
  6.5 15.9 %copy-start = (s32[4,2]{0,1:T(2,128)S(1)}, s32[4,2]{0,1:T(2,128)}, u32[]{:S(2)}) copy-start(s32[4,2]{0,1:T(2,128)} %param.11) | copy-start | bytes 100
  6.5 32.3 %all-gather.2.cloned.1.call-start = ((), (), s32[]{:S(2)}) async-start(), calls=%async_computation | async-start | bytes 1556480 | tf_op jit(solution)/shard_map/all_gather | solution.py:97
  7.3 6.4 %collective-permute-start = (f32[10,512]{1,0:T(8,128)S(1)}, f32[10,512]{1,0:T(8,128)S(1)}, u32[]{:S(2)}, u32[]{:S(2)}) collective-permute-start(f32[10,512]{1,0:T(8,128)S(1)} %get-tuple-element.5), channel_id=1, source_target_pairs={{0,4},{4,8},{8,12},{12,16},{16,20},{20,24},{24,28},{1,5},{5,9},{9,... | collective-permute-start | bytes 61448 | tf_op jit(solution)/shard_map/ppermute | solution.py:94
  12.2 5.8 %collective-permute-start.1 = (f32[10,512]{1,0:T(8,128)S(1)}, f32[10,512]{1,0:T(8,128)S(1)}, u32[]{:S(2)}, u32[]{:S(2)}) collective-permute-start(f32[10,512]{1,0:T(8,128)S(1)} %get-tuple-element.6), channel_id=1, source_target_pairs={{4,0},{8,4},{12,8},{16,12},{20,16},{24,20},{28,24},{5,1},{9,5},{13... | collective-permute-start | bytes 61448 | tf_op jit(solution)/shard_map/ppermute | solution.py:95
  22.4 17.8 %copy-start.1 = (f32[1,128,2048]{2,1,0:T(8,128)S(1)}, f32[1,128,2048]{2,1,0:T(8,128)}, u32[]{:S(2)}) copy-start(f32[1,128,2048]{2,1,0:T(8,128)} %param.10) | copy-start | bytes 3145732
Sparse Core Ops, SparseCore 0:
  19.9 18.9 all-gather.1

commit v2 on v1

v2 whole, which is shorter than its diff:
```python
import functools

import jax
import jax.numpy as jnp
from jax import lax
from jax.experimental import pallas as pl
from jax.experimental.pallas import tpu as pltpu
from jax.sharding import PartitionSpec as P

BLOCK = 64
WINDOW = 96
HALO = 16
LANES = 128
CHUNK = 256
MESH = pl.DeviceIdType.MESH


def split(value):
    high = value.astype(jnp.bfloat16)
    low = (value - high.astype(jnp.float32)).astype(jnp.bfloat16)
    return high, low


def kernel(
    tiles, visits, row_ref, col_ref, coeff_ref, boxes_ref, own_ref, vis_ref, out_ref,
    t_ref, w_ref, even_ref, odd_ref, send_sem, recv_sem,
):
    taps = row_ref.shape[1]
    half = taps // 2
    rows, width = own_ref.shape
    columns = width * visits
    steps = columns // CHUNK
    blocks = rows // BLOCK
    depth = w_ref.shape[3]
    tile, visit = lax.axis_index("tile"), lax.axis_index("visit")
    forward = visit < visits // 2
    above, below = tile > 0, tile < tiles - 1

    def span(owner):
        return pl.ds(pl.multiple_of(LANES + owner * width, LANES), width)

    def copy(kind, peer, owner):
        source, first, count, to = (
            (own_ref, HALO, rows, tile),
            (own_ref.at[pl.ds(rows - HALO, HALO)], 0, HALO, tile + 1),
            (own_ref.at[pl.ds(0, HALO)], HALO + rows, HALO, tile - 1),
        )[kind]
        return pltpu.make_async_remote_copy(
            src_ref=source,
            dst_ref=t_ref.at[pl.ds(first, count), span(owner)],
            send_sem=send_sem.at[kind, peer],
            recv_sem=recv_sem.at[kind, owner],
            device_id=(to, peer),
            device_id_type=MESH,
        )

    barrier = pltpu.get_barrier_semaphore()

    def greet(to, peer):
        pl.semaphore_signal(barrier, inc=1, device_id=(to, peer), device_id_type=MESH)

    for offset in range(1, visits):
        greet(tile, lax.rem(visit + offset, visits))
    for allowed, to in ((above, tile - 1), (below, tile + 1)):
        @pl.when(allowed)
        def _():
            for peer in range(visits):
                greet(to, peer)
    beside = jnp.where(above, 1, 0) + jnp.where(below, 1, 0)
    pl.semaphore_wait(barrier, visits - 1 + visits * beside)

    for offset in range(1, visits):
        copy(0, lax.rem(visit + offset, visits), visit).start()
    for kind, allowed in ((1, below), (2, above)):
        @pl.when(allowed)
        def _():
            for peer in range(visits):
                copy(kind, peer, visit).start()

    t_ref[HALO : HALO + rows, span(visit)] = own_ref[...]
    side = jnp.zeros((t_ref.shape[0], LANES), jnp.float32)
    t_ref[:, :LANES] = side
    t_ref[:, LANES + columns :] = side
    for allowed, first in ((above, 0), (below, HALO + rows)):
        @pl.when(jnp.logical_not(allowed))
        def _():
            t_ref[first : first + HALO, LANES : LANES + columns] = jnp.zeros(
                (HALO, columns), jnp.float32
            )

    exact = functools.partial(
        lax.dot_general, precision=lax.Precision.HIGHEST, preferred_element_type=jnp.float32
    )
    place = lax.broadcasted_iota(jnp.int32, (1, depth), 1)
    group = jnp.zeros_like(place)
    for b in range(1, taps + 1):
        group = group + jnp.where(place >= b * WINDOW, 1, 0)
    tap = lax.broadcasted_iota(jnp.int32, (taps, depth), 0)
    in_rows = jnp.where(tap == place - group * WINDOW - (HALO - half), 1.0, 0.0)
    in_cols = jnp.where(tap == group, 1.0, 0.0)
    plain = (((1,), (0,)), ((), ()))
    products = exact(row_ref[...], in_rows, plain) * exact(col_ref[...], in_cols, plain)
    base = exact(coeff_ref[0], products, (((0,), (0,)), ((), ())))
    rolled = [
        pltpu.roll(jnp.broadcast_to(base[t : t + 1], (BLOCK, depth)), 0, 1, stride=1, stride_axis=0)
        for t in range(6)
    ]
    for block in range(blocks):
        row = lax.broadcasted_iota(jnp.int32, (BLOCK, 1), 0) + (tile * rows + block * BLOCK)
        y = 2.0 * (row.astype(jnp.float32) + 0.5) / (rows * tiles) - 1.0
        parts = (
            rolled[0] + y * (rolled[2] + y * rolled[5]),
            rolled[1] + y * rolled[4],
            rolled[3],
        )
        for i, part in enumerate(parts):
            high, low = split(part)
            w_ref[0, block, i * BLOCK : (i + 1) * BLOCK, :] = high
            w_ref[1, block, i * BLOCK : (i + 1) * BLOCK, :] = low
    pad = depth - taps * WINDOW
    if pad:
        for s_ref in (even_ref, odd_ref):
            s_ref[:, :, taps * WINDOW :, :] = jnp.zeros((2, blocks, pad, CHUNK), jnp.bfloat16)

    first_column = boxes_ref[visit, 0]
    end_column = first_column + boxes_ref[visit, 1]

    def chunk_of(step):
        return jnp.where(forward, step, steps - 1 - step)

    def arrive(step):
        for order in range(visits):
            needed = max(0, -(-(order * width - half + 1) // CHUNK) - 1)
            owner = jnp.where(forward, order, visits - 1 - order)
            for kind, allowed in ((0, owner != visit), (1, above), (2, below)):
                @pl.when(jnp.logical_and(step == needed, allowed))
                def _():
                    copy(kind, visit, owner).wait_recv()

    def build(step, s_ref):
        start = pl.multiple_of(chunk_of(step) * CHUNK, CHUNK)
        window = t_ref[:, pl.ds(start, CHUNK + 2 * LANES)]
        for which, part in enumerate(split(window)):
            for b in range(taps):
                first = LANES - half + b
                shifted = part[:, first : first + CHUNK]
                for block in range(blocks):
                    s_ref[which, block, b * WINDOW : (b + 1) * WINDOW, :] = shifted[
                        block * BLOCK : block * BLOCK + WINDOW
                    ]

    def finish(step, s_ref):
        start = pl.multiple_of(chunk_of(step) * CHUNK, CHUNK)
        column = lax.broadcasted_iota(jnp.int32, (1, CHUNK), 1) + start
        x = 2.0 * (column.astype(jnp.float32) + 0.5) / columns - 1.0
        inside = (column >= first_column) & (column < end_column)
        dot = functools.partial(jnp.dot, preferred_element_type=jnp.float32)
        for block in range(blocks):
            total = (
                dot(w_ref[0, block], s_ref[0, block])
                + dot(w_ref[1, block], s_ref[0, block])
                + dot(w_ref[0, block], s_ref[1, block])
            )
            model = total[:BLOCK] + x * (total[BLOCK : 2 * BLOCK] + x * total[2 * BLOCK :])
            at = slice(block * BLOCK, (block + 1) * BLOCK)
            out_ref[at, pl.ds(start, CHUNK)] = jnp.where(
                inside, vis_ref[at, pl.ds(start, CHUNK)] - model, 0.0
            )

    arrive(0)
    build(0, even_ref)

    def pair(index, carry):
        step = 2 * index
        arrive(step + 1)
        build(step + 1, odd_ref)
        finish(step, even_ref)
        arrive(step + 2)
        build(jnp.minimum(step + 2, steps - 1), even_ref)
        finish(step + 1, odd_ref)
        return carry

    lax.fori_loop(0, steps // 2, pair, 0)

    for offset in range(1, visits):
        copy(0, lax.rem(visit + offset, visits), visit).wait_send()
    for kind, allowed in ((1, below), (2, above)):
        @pl.when(allowed)
        def _():
            for peer in range(visits):
                copy(kind, peer, visit).wait_send()


def local(template, row_taps, col_taps, coeffs, visits, boxes):
    taps = row_taps.shape[1]
    rows, width = template.shape
    peers = lax.axis_size("visit")
    columns = width * peers
    blocks = rows // BLOCK
    depth = -(-taps * WINDOW // 256) * 256
    vmem = pl.BlockSpec(memory_space=pltpu.VMEM)
    out = pl.pallas_call(
        functools.partial(kernel, lax.axis_size("tile"), peers),
        in_specs=[vmem, vmem, vmem, pl.BlockSpec(memory_space=pltpu.SMEM), vmem, vmem],
        out_specs=vmem,
        out_shape=jax.ShapeDtypeStruct((rows, columns), jnp.float32),
        scratch_shapes=[
            pltpu.VMEM((rows + 2 * HALO, columns + 2 * LANES), jnp.float32),
            pltpu.VMEM((2, blocks, 3 * BLOCK, depth), jnp.bfloat16),
            pltpu.VMEM((2, blocks, depth, CHUNK), jnp.bfloat16),
            pltpu.VMEM((2, blocks, depth, CHUNK), jnp.bfloat16),
            pltpu.SemaphoreType.DMA((3, peers)),
            pltpu.SemaphoreType.DMA((3, peers)),
        ],
        compiler_params=pltpu.CompilerParams(
            collective_id=0, has_side_effects=True, vmem_limit_bytes=50 * 2**20
        ),
    )(row_taps, col_taps, coeffs, boxes, template, visits[0])
    return out[None]


def solution(mesh):
    placed = (P("tile", "visit"), P(), P(), P("visit", None, None), P("visit", "tile", None), P())
    return jax.shard_map(
        local, mesh=mesh, in_specs=placed, out_specs=P("visit", "tile", None), check_vma=False
    )
```

time: 67 us -> 35.8 us (0.53)
  waiting for transfers between devices: 18.4 us -> 0 us
  between operations: 14.7 us -> 0.02 us
  Pallas kernels: 19.4 us -> 30.6 us
  starting transfers between devices: 6.15 us -> 0 us
  other arithmetic: 3.45 us -> 0 us
    all_gather x1 -> x0, waiting for transfers between devices: 13.9 us -> none  [local(): slab = lax.all_gather(slab, 'visit', axis=1, tiled=True)]
    pallas_call x1, Pallas kernels: 19.4 us -> 30.6 us  [local(): pl.pallas_call(functools.partial(kernel, lax.axis_size('tile'), peers), i...]
    ppermute x2 -> x0, starting transfers between devices: 6.15 us -> none  [the longest x1 4.86 us: local(): lax.ppermute(template[rows - half:], 'tile', [(i, i + 1) for i in range(c...]
    ppermute x2 -> x0, waiting for transfers between devices: 4.51 us -> none  [the longest x1 4.23 us: local(): lax.ppermute(template[:half], 'tile', [(i + 1, i) for i in range(count -...]
    unnamed x6 -> x15, local copies, waits for them, and re-layouts: 1.48 us -> 4.7 us
    concatenate x1 -> x0, other arithmetic: 1.71 us -> none  [local(): slab = jnp.concatenate([above, template, below], axis=0)]
    pad x3 -> x0, local copies, waits for them, and re-layouts: 1.41 us -> none  [the longest x1 1.39 us: local(): slab = jnp.pad(slab, ((0, tall - slab.shape[0]), (LANES, LANES)))]
    slice x2 -> x0, local copies, waits for them, and re-layouts: 1.38 us -> none  [the longest x1 0.79 us: local(): template[rows - half:]]
  transfers between devices with their start and end apart: 3 -> 0, of which waited for: 3 -> 0; matrix products, arithmetic and copies ran while one was open for 6% -> 0% of each run, Pallas kernels for 0% -> 0%
where the time goes in v2:
time: 35.8 us; the launch traced here: 35.3 us
  Pallas kernels  30.6 us (85%)
  local copies, waits for them, and re-layouts  4.7 us (13%)
    pallas_call x1, Pallas kernels, local(): pl.pallas_call(functools.partial(kernel, lax.axis_size('tile'), peers), i...  30.6 us
    unnamed x15, local copies, waits for them, and re-layouts  4.7 us

profile of v2, /device:TPU:0, one launch (start us, length us, event | category | flops | bytes accessed | tf_op | source)
XLA Modules:
  0.0 35.3 jit_solution(11699209891829397956)
XLA Ops:
  0.0 0.0 copy-start.5
  0.0 0.0 copy-start.4
  0.0 0.0 copy-start.2
  0.0 0.7 %copy-done.5 = s32[4,2]{0,1:T(2,128)S(1)} copy-done((s32[4,2]{0,1:T(2,128)S(1)}, s32[4,2]{0,1:T(2,128)}, u32[]{:S(2)}) %copy-start.5) | copy-done | bytes 56
  0.7 0.1 copy.8.boxes_ref
  0.8 0.0 copy-done.4
  0.8 0.1 copy.7.coeff_ref
  0.9 0.0 copy-done.2
  0.9 0.0 copy-start
  0.9 1.2 %copy-done = f32[1,128,2048]{2,1,0:T(8,128)S(1)} copy-done((f32[1,128,2048]{2,1,0:T(8,128)S(1)}, f32[1,128,2048]{2,1,0:T(8,128)}, u32[]{:S(2)}) %copy-start) | copy-done | bytes 1048600
  2.1 0.0 copy-start.1
  2.1 0.9 %copy-done.1 = f32[128,512]{1,0:T(8,128)S(1)} copy-done((f32[128,512]{1,0:T(8,128)S(1)}, f32[128,512]{1,0:T(8,128)}, u32[]{:S(2)}) %copy-start.1) | copy-done | bytes 262168
  3.0 0.0 copy-start.3
  3.0 0.7 %copy-done.3 = f32[16,21]{1,0:T(8,128)S(1)} copy-done((f32[16,21]{1,0:T(8,128)S(1)}, f32[16,21]{1,0:T(8,128)}, u32[]{:S(2)}) %copy-start.3) | copy-done | bytes 1368
  3.7 30.6 %shard_map.64 = f32[128,2048]{1,0:T(8,128)S(1)} custom-call(f32[16,21]{1,0:T(8,128)S(1)} %copy-done.2, f32[16,21]{1,0:T(8,128)S(1)} %copy-done.3, f32[1,16,6]{2,1,0:T(8,128)S(1)} %copy.7.coeff_ref, s32[4,2]{1,0:T(4,128)S(1)} %copy.8.boxes_ref, f32[128,512]{1,0:T(8,128)S(1)} %copy-done.1, f32[128,2048]{1,0:T(8,128)S(1)} %bitcast.3), custom_call_target="tpu_custom_call" | custom-call | tf_op jit(solution)/shard_map/pallas_call | solution.py:202
  34.3 1.0 %copy.10 = f32[1,128,2048]{2,1,0:T(8,128)} copy(f32[1,128,2048]{2,1,0:T(8,128)S(1)} %bitcast.2) | data formatting | bytes 2097152
Async XLA Ops:
  0.0 0.7 %copy-start.5 = (s32[4,2]{0,1:T(2,128)S(1)}, s32[4,2]{0,1:T(2,128)}, u32[]{:S(2)}) copy-start(s32[4,2]{0,1:T(2,128)} %param.11) | copy-start | bytes 100
  0.0 0.8 %copy-start.4 = (f32[1,16,6]{1,0,2:T(1,128)S(1)}, f32[1,16,6]{1,0,2:T(1,128)}, u32[]{:S(2)}) copy-start(f32[1,16,6]{1,0,2:T(1,128)} %param.9) | copy-start | bytes 1156
  0.0 0.9 %copy-start.2 = (f32[16,21]{1,0:T(8,128)S(1)}, f32[16,21]{1,0:T(8,128)}, u32[]{:S(2)}) copy-start(f32[16,21]{1,0:T(8,128)} %row_ref.1) | copy-start | bytes 4036
  0.9 1.2 %copy-start = (f32[1,128,2048]{2,1,0:T(8,128)S(1)}, f32[1,128,2048]{2,1,0:T(8,128)}, u32[]{:S(2)}) copy-start(f32[1,128,2048]{2,1,0:T(8,128)} %param.10) | copy-start | bytes 3145732
  2.1 0.9 %copy-start.1 = (f32[128,512]{1,0:T(8,128)S(1)}, f32[128,512]{1,0:T(8,128)}, u32[]{:S(2)}) copy-start(f32[128,512]{1,0:T(8,128)} %own_ref.1) | copy-start | bytes 786436
  3.0 0.7 %copy-start.3 = (f32[16,21]{1,0:T(8,128)S(1)}, f32[16,21]{1,0:T(8,128)}, u32[]{:S(2)}) copy-start(f32[16,21]{1,0:T(8,128)} %col_ref.1) | copy-start | bytes 4036

commit v3 on v2

v3 whole, which is shorter than its diff:
```python
import functools

import jax
import jax.numpy as jnp
from jax import lax
from jax.experimental import pallas as pl
from jax.experimental.pallas import tpu as pltpu
from jax.sharding import PartitionSpec as P

BLOCK = 64
WINDOW = 96
HALO = 16
LANES = 128
CHUNK = 256
MESH = pl.DeviceIdType.MESH


def split(value):
    high = value.astype(jnp.bfloat16)
    low = (value - high.astype(jnp.float32)).astype(jnp.bfloat16)
    return high, low


def kernel(
    tiles, visits, row_hbm, col_hbm, coeff_hbm, boxes_ref, own_hbm, vis_hbm, out_ref,
    row_ref, col_ref, coeff_ref, vis_ref, t_ref, w_ref, even_ref, odd_ref,
    local_sem, send_sem, recv_sem,
):
    taps = row_ref.shape[1]
    half = taps // 2
    rows, width = own_hbm.shape
    columns = width * visits
    steps = columns // CHUNK
    blocks = rows // BLOCK
    depth = w_ref.shape[2]
    stack = 3 * BLOCK
    tile, visit = lax.axis_index("tile"), lax.axis_index("visit")
    forward = visit < visits // 2
    above, below = tile > 0, tile < tiles - 1
    chips = visits // 2
    core, chip = lax.rem(visit, 2), visit // 2
    partner = chip * 2 + 1 - core
    across = [lax.rem(chip + hop, chips) * 2 + core for hop in range(1, chips)]
    kinds = ((0, None), (1, above), (2, below))
    late = chips == 2 and 2 * width - half >= 2 * CHUNK

    def guarded(condition, action):
        if condition is None:
            action()
        else:
            pl.when(condition)(action)

    def piece(kind, owner):
        first, count = ((HALO, rows), (0, HALO), (HALO + rows, HALO))[kind]
        return t_ref.at[
            pl.ds(first, count), pl.ds(pl.multiple_of(LANES + owner * width, LANES), width)
        ]

    def copy(kind, source, owner, sem, to, peer):
        return pltpu.make_async_remote_copy(
            src_ref=source,
            dst_ref=piece(kind, owner),
            send_sem=sem,
            recv_sem=recv_sem.at[kind, owner],
            device_id=(to, peer),
            device_id_type=MESH,
        )

    def spread(kind, peer):
        source = own_hbm if kind == 0 else piece(kind, visit)
        return copy(kind, source, visit, send_sem.at[kind, peer], tile, peer)

    def edge(kind):
        source = own_hbm.at[pl.ds(rows - HALO if kind == 1 else 0, HALO)]
        to = tile + 1 if kind == 1 else tile - 1
        return copy(kind, source, visit, send_sem.at[kind, visit], to, visit)

    def onward(kind, owner):
        return copy(kind, piece(kind, owner), owner, send_sem.at[3 + kind, owner], tile, partner)

    def arrived(kind, owner):
        copy(kind, piece(kind, owner), owner, send_sem.at[kind, owner], tile, partner).wait_recv()

    loads = [
        pltpu.make_async_copy(source, target, local_sem.at[at])
        for at, (source, target) in enumerate((
            (row_hbm, row_ref), (col_hbm, col_ref), (coeff_hbm, coeff_ref),
            (own_hbm, piece(0, visit)), (vis_hbm, vis_ref),
        ))
    ]
    for load in loads:
        load.start()

    barrier = pltpu.get_barrier_semaphore()

    def greet(to, peer):
        pl.semaphore_signal(barrier, inc=1, device_id=(to, peer), device_id_type=MESH)

    for peer in [*across, partner]:
        greet(tile, peer)
    pl.when(above)(lambda: greet(tile - 1, visit))
    pl.when(below)(lambda: greet(tile + 1, visit))
    beside = jnp.where(above, 1, 0) + jnp.where(below, 1, 0)
    pl.semaphore_wait(barrier, chips + beside)

    pl.when(below)(lambda: edge(1).start())
    pl.when(above)(lambda: edge(2).start())
    for peer in [*across, partner]:
        spread(0, peer).start()

    side = jnp.zeros((t_ref.shape[0], LANES), jnp.float32)
    t_ref[:, :LANES] = side
    t_ref[:, LANES + columns :] = side
    for allowed, first in ((above, 0), (below, HALO + rows)):
        @pl.when(jnp.logical_not(allowed))
        def _():
            t_ref[first : first + HALO, LANES : LANES + columns] = jnp.zeros(
                (HALO, columns), jnp.float32
            )
    for load in loads:
        load.wait()

    exact = functools.partial(
        lax.dot_general, precision=lax.Precision.HIGHEST, preferred_element_type=jnp.float32
    )
    place = lax.broadcasted_iota(jnp.int32, (1, depth), 1)
    group = jnp.zeros_like(place)
    for b in range(1, taps + 1):
        group = group + jnp.where(place >= b * WINDOW, 1, 0)
    tap = lax.broadcasted_iota(jnp.int32, (taps, depth), 0)
    in_rows = jnp.where(tap == place - group * WINDOW - (HALO - half), 1.0, 0.0)
    in_cols = jnp.where(tap == group, 1.0, 0.0)
    plain = (((1,), (0,)), ((), ()))
    products = exact(row_ref[...], in_rows, plain) * exact(col_ref[...], in_cols, plain)
    base = exact(coeff_ref[0], products, (((0,), (0,)), ((), ())))
    for kind, allowed in kinds[1:]:
        @pl.when(allowed)
        def _():
            arrived(kind, visit)
            for peer in [*across, partner]:
                spread(kind, peer).start()
    rolled = [
        pltpu.roll(jnp.broadcast_to(base[t : t + 1], (BLOCK, depth)), 0, 1, stride=1, stride_axis=0)
        for t in range(6)
    ]
    for block in range(blocks):
        row = lax.broadcasted_iota(jnp.int32, (BLOCK, 1), 0) + (tile * rows + block * BLOCK)
        y = 2.0 * (row.astype(jnp.float32) + 0.5) / (rows * tiles) - 1.0
        parts = (
            rolled[0] + y * (rolled[2] + y * rolled[5]),
            rolled[1] + y * rolled[4],
            rolled[3],
        )
        for i, part in enumerate(parts):
            high, low = split(part)
            w_ref[block, i * BLOCK : (i + 1) * BLOCK, :] = high
            w_ref[block, stack + i * BLOCK : stack + (i + 1) * BLOCK, :] = low
    pad = depth - taps * WINDOW
    if pad:
        for s_ref in (even_ref, odd_ref):
            s_ref[:, :, taps * WINDOW :, :] = jnp.zeros((2, blocks, pad, CHUNK), jnp.bfloat16)

    first_column = boxes_ref[visit, 0]
    end_column = first_column + boxes_ref[visit, 1]

    def chunk_of(step):
        return jnp.where(forward, step, steps - 1 - step)

    def arrive(step):
        for order in range(visits):
            needed = max(0, -(-(order * width - half + 1) // CHUNK) - 1)
            owner = jnp.where(forward, order, visits - 1 - order)
            for kind, allowed in kinds:
                here = jnp.logical_and(step == needed, lax.rem(owner, 2) != core)
                if allowed is not None:
                    here = jnp.logical_and(here, allowed)
                pl.when(here)(functools.partial(arrived, kind, owner))

    def relay():
        for owner in across:
            for kind, allowed in kinds:
                def pass_on():
                    arrived(kind, owner)
                    onward(kind, owner).start()
                guarded(allowed, pass_on)

    def build(step, s_ref):
        start = pl.multiple_of(chunk_of(step) * CHUNK, CHUNK)
        window = t_ref[:, pl.ds(start, CHUNK + 2 * LANES)]
        for which, part in enumerate(split(window)):
            for b in range(taps):
                first = LANES - half + b
                shifted = part[:, first : first + CHUNK]
                for block in range(blocks):
                    s_ref[which, block, b * WINDOW : (b + 1) * WINDOW, :] = shifted[
                        block * BLOCK : block * BLOCK + WINDOW
                    ]

    def finish(step, s_ref):
        start = pl.multiple_of(chunk_of(step) * CHUNK, CHUNK)
        column = lax.broadcasted_iota(jnp.int32, (1, CHUNK), 1) + start
        x = 2.0 * (column.astype(jnp.float32) + 0.5) / columns - 1.0
        inside = (column >= first_column) & (column < end_column)
        dot = functools.partial(jnp.dot, preferred_element_type=jnp.float32)
        for block in range(blocks):
            both = dot(w_ref[block], s_ref[0, block])
            total = both[:stack] + both[stack:] + dot(w_ref[block, :stack], s_ref[1, block])
            model = total[:BLOCK] + x * (total[BLOCK : 2 * BLOCK] + x * total[2 * BLOCK :])
            at = slice(block * BLOCK, (block + 1) * BLOCK)
            out_ref[at, pl.ds(start, CHUNK)] = jnp.where(
                inside, vis_ref[at, pl.ds(start, CHUNK)] - model, 0.0
            )

    if not late:
        relay()
    arrive(0)
    build(0, even_ref)

    def pair(index, carry):
        step = 2 * index
        arrive(step + 1)
        build(step + 1, odd_ref)
        finish(step, even_ref)
        if late:
            pl.when(index == 0)(relay)
        arrive(step + 2)
        build(jnp.minimum(step + 2, steps - 1), even_ref)
        finish(step + 1, odd_ref)
        return carry

    lax.fori_loop(0, steps // 2, pair, 0)

    pl.when(below)(lambda: edge(1).wait_send())
    pl.when(above)(lambda: edge(2).wait_send())
    for kind, allowed in kinds:
        def sent():
            for peer in [*across, partner]:
                spread(kind, peer).wait_send()
            for owner in across:
                onward(kind, owner).wait_send()
        guarded(allowed, sent)


def local(template, row_taps, col_taps, coeffs, visits, boxes):
    taps = row_taps.shape[1]
    rows, width = template.shape
    peers = lax.axis_size("visit")
    columns = width * peers
    blocks = rows // BLOCK
    depth = -(-taps * WINDOW // 256) * 256
    hbm = pl.BlockSpec(memory_space=pltpu.HBM)
    out = pl.pallas_call(
        functools.partial(kernel, lax.axis_size("tile"), peers),
        in_specs=[hbm, hbm, hbm, pl.BlockSpec(memory_space=pltpu.SMEM), hbm, hbm],
        out_specs=pl.BlockSpec(memory_space=pltpu.VMEM),
        out_shape=jax.ShapeDtypeStruct((rows, columns), jnp.float32),
        scratch_shapes=[
            pltpu.VMEM(row_taps.shape, jnp.float32),
            pltpu.VMEM(col_taps.shape, jnp.float32),
            pltpu.VMEM(coeffs.shape, jnp.float32),
            pltpu.VMEM((rows, columns), jnp.float32),
            pltpu.VMEM((rows + 2 * HALO, columns + 2 * LANES), jnp.float32),
            pltpu.VMEM((blocks, 6 * BLOCK, depth), jnp.bfloat16),
            pltpu.VMEM((2, blocks, depth, CHUNK), jnp.bfloat16),
            pltpu.VMEM((2, blocks, depth, CHUNK), jnp.bfloat16),
            pltpu.SemaphoreType.DMA((5,)),
            pltpu.SemaphoreType.DMA((6, peers)),
            pltpu.SemaphoreType.DMA((3, peers)),
        ],
        compiler_params=pltpu.CompilerParams(
            collective_id=0, has_side_effects=True, vmem_limit_bytes=62 * 2**20
        ),
    )(row_taps, col_taps, coeffs, boxes, template, visits[0])
    return out[None]


def solution(mesh):
    placed = (P("tile", "visit"), P(), P(), P("visit", None, None), P("visit", "tile", None), P())
    return jax.shard_map(
        local, mesh=mesh, in_specs=placed, out_specs=P("visit", "tile", None), check_vma=False
    )
```

time: 35.8 us -> 30.9 us (0.86)
  Pallas kernels: 30.6 us -> 26.3 us
  local copies, waits for them, and re-layouts: 4.7 us -> 4.3 us
    pallas_call x1, Pallas kernels: 30.6 us -> 26.3 us  [local(): pl.pallas_call(functools.partial(kernel, lax.axis_size('tile'), peers), i...]
    unnamed x15 -> x7, local copies, waits for them, and re-layouts: 4.7 us -> 4.3 us
where the time goes in v3:
time: 30.9 us; the launch traced here: 30.7 us
  Pallas kernels  26.3 us (85%)
  local copies, waits for them, and re-layouts  4.3 us (14%)
    pallas_call x1, Pallas kernels, local(): pl.pallas_call(functools.partial(kernel, lax.axis_size('tile'), peers), i...  26.3 us
    unnamed x7, local copies, waits for them, and re-layouts  4.3 us

profile of v3, /device:TPU:0, one launch (start us, length us, event | category | flops | bytes accessed | tf_op | source)
XLA Modules:
  0.0 30.7 jit_solution(14136666977421073039)
XLA Ops:
  0.0 0.0 copy-start.1
  0.0 0.0 copy-start
  0.0 0.7 %copy-done.1 = s32[4,2]{0,1:T(2,128)S(1)} copy-done((s32[4,2]{0,1:T(2,128)S(1)}, s32[4,2]{0,1:T(2,128)}, u32[]{:S(2)}) %copy-start.1) | copy-done | bytes 56
  0.7 0.6 %copy.8.boxes_ref = s32[4,2]{1,0:T(4,128)} copy(s32[4,2]{0,1:T(2,128)S(1)} %copy-done.1) | data formatting | bytes 64 | tf_op args[5]
  1.3 0.0 copy-done
  1.3 0.7 %copy.7.coeff_hbm = f32[1,16,6]{2,1,0:T(8,128)} copy(f32[1,16,6]{1,0,2:T(1,128)S(1)} %copy-done) | data formatting | bytes 768 | tf_op args[3]
  2.0 26.3 %shard_map.64 = f32[128,2048]{1,0:T(8,128)} custom-call(f32[16,21]{1,0:T(8,128)} %row_hbm.1, f32[16,21]{1,0:T(8,128)} %col_hbm.1, f32[1,16,6]{2,1,0:T(8,128)} %copy.7.coeff_hbm, s32[4,2]{1,0:T(4,128)} %copy.8.boxes_ref, f32[128,512]{1,0:T(8,128)} %own_hbm.1, f32[128,2048]{1,0:T(8,128)} %bitcast.3), custom_call_target="tpu_custom_call" | custom-call | tf_op jit(solution)/shard_map/pallas_call | solution.py:252
  28.4 2.3 %copy.10 = f32[1,128,2048]{2,1,0:T(8,128)} copy(f32[1,128,2048]{2,1,0:T(8,128)} %bitcast.2) | data formatting | bytes 2097152
Async XLA Ops:
  0.0 0.7 %copy-start.1 = (s32[4,2]{0,1:T(2,128)S(1)}, s32[4,2]{0,1:T(2,128)}, u32[]{:S(2)}) copy-start(s32[4,2]{0,1:T(2,128)} %param.11) | copy-start | bytes 100
  0.0 1.3 %copy-start = (f32[1,16,6]{1,0,2:T(1,128)S(1)}, f32[1,16,6]{1,0,2:T(1,128)}, u32[]{:S(2)}) copy-start(f32[1,16,6]{1,0,2:T(1,128)} %param.9) | copy-start | bytes 1156

commit v4 on v3

--- a/solution.py
+++ b/solution.py
@@ -22,8 +22,8 @@
 
 
 def kernel(
-    tiles, visits, row_hbm, col_hbm, coeff_hbm, boxes_ref, own_hbm, vis_hbm, out_ref,
-    row_ref, col_ref, coeff_ref, vis_ref, t_ref, w_ref, even_ref, odd_ref,
+    tiles, visits, row_hbm, col_hbm, coeff_hbm, own_hbm, out_ref,
+    row_ref, col_ref, coeff_ref, t_ref, w_ref, even_ref, odd_ref,
     local_sem, send_sem, recv_sem,
 ):
     taps = row_ref.shape[1]
@@ -85,7 +85,7 @@
         pltpu.make_async_copy(source, target, local_sem.at[at])
         for at, (source, target) in enumerate((
             (row_hbm, row_ref), (col_hbm, col_ref), (coeff_hbm, coeff_ref),
-            (own_hbm, piece(0, visit)), (vis_hbm, vis_ref),
+            (own_hbm, piece(0, visit)),
         ))
     ]
     for load in loads:
@@ -132,7 +132,7 @@
     in_cols = jnp.where(tap == group, 1.0, 0.0)
     plain = (((1,), (0,)), ((), ()))
     products = exact(row_ref[...], in_rows, plain) * exact(col_ref[...], in_cols, plain)
-    base = exact(coeff_ref[0], products, (((0,), (0,)), ((), ())))
+    base = exact(coeff_ref[:, 0, :], products, plain)
     for kind, allowed in kinds[1:]:
         @pl.when(allowed)
         def _():
@@ -160,9 +160,6 @@
         for s_ref in (even_ref, odd_ref):
             s_ref[:, :, taps * WINDOW :, :] = jnp.zeros((2, blocks, pad, CHUNK), jnp.bfloat16)
 
-    first_column = boxes_ref[visit, 0]
-    end_column = first_column + boxes_ref[visit, 1]
-
     def chunk_of(step):
         return jnp.where(forward, step, steps - 1 - step)
 
@@ -200,16 +197,13 @@
         start = pl.multiple_of(chunk_of(step) * CHUNK, CHUNK)
         column = lax.broadcasted_iota(jnp.int32, (1, CHUNK), 1) + start
         x = 2.0 * (column.astype(jnp.float32) + 0.5) / columns - 1.0
-        inside = (column >= first_column) & (column < end_column)
         dot = functools.partial(jnp.dot, preferred_element_type=jnp.float32)
         for block in range(blocks):
             both = dot(w_ref[block], s_ref[0, block])
             total = both[:stack] + both[stack:] + dot(w_ref[block, :stack], s_ref[1, block])
             model = total[:BLOCK] + x * (total[BLOCK : 2 * BLOCK] + x * total[2 * BLOCK :])
             at = slice(block * BLOCK, (block + 1) * BLOCK)
-            out_ref[at, pl.ds(start, CHUNK)] = jnp.where(
-                inside, vis_ref[at, pl.ds(start, CHUNK)] - model, 0.0
-            )
+            out_ref[at, pl.ds(start, CHUNK)] = model
 
     if not late:
         relay()
@@ -249,29 +243,31 @@
     blocks = rows // BLOCK
     depth = -(-taps * WINDOW // 256) * 256
     hbm = pl.BlockSpec(memory_space=pltpu.HBM)
-    out = pl.pallas_call(
+    model = pl.pallas_call(
         functools.partial(kernel, lax.axis_size("tile"), peers),
-        in_specs=[hbm, hbm, hbm, pl.BlockSpec(memory_space=pltpu.SMEM), hbm, hbm],
+        in_specs=[hbm] * 4,
         out_specs=pl.BlockSpec(memory_space=pltpu.VMEM),
         out_shape=jax.ShapeDtypeStruct((rows, columns), jnp.float32),
         scratch_shapes=[
             pltpu.VMEM(row_taps.shape, jnp.float32),
             pltpu.VMEM(col_taps.shape, jnp.float32),
-            pltpu.VMEM(coeffs.shape, jnp.float32),
-            pltpu.VMEM((rows, columns), jnp.float32),
+            pltpu.VMEM((coeffs.shape[2], 1, coeffs.shape[1]), jnp.float32),
             pltpu.VMEM((rows + 2 * HALO, columns + 2 * LANES), jnp.float32),
             pltpu.VMEM((blocks, 6 * BLOCK, depth), jnp.bfloat16),
             pltpu.VMEM((2, blocks, depth, CHUNK), jnp.bfloat16),
             pltpu.VMEM((2, blocks, depth, CHUNK), jnp.bfloat16),
-            pltpu.SemaphoreType.DMA((5,)),
+            pltpu.SemaphoreType.DMA((4,)),
             pltpu.SemaphoreType.DMA((6, peers)),
             pltpu.SemaphoreType.DMA((3, peers)),
         ],
         compiler_params=pltpu.CompilerParams(
             collective_id=0, has_side_effects=True, vmem_limit_bytes=62 * 2**20
         ),
-    )(row_taps, col_taps, coeffs, boxes, template, visits[0])
-    return out[None]
+    )(row_taps, col_taps, coeffs.transpose(2, 0, 1), template)
+    box = lax.dynamic_slice_in_dim(boxes, lax.axis_index("visit"), 1, 0)
+    column = jnp.arange(columns)[None, :]
+    inside = (column >= box[:, 0:1]) & (column < box[:, 0:1] + box[:, 1:2])
+    return jnp.where(inside[:, None, :], visits - model[None], jnp.float32(0.0))
 
 
 def solution(mesh):

time: 30.9 us -> 31.5 us (1.019)
  other arithmetic: 0 us -> 3.04 us
  local copies, waits for them, and re-layouts: 4.3 us -> 1.33 us
  between operations: 0.01 us -> 1.31 us
  Pallas kernels: 26.3 us -> 25.6 us
    unnamed x7 -> x4, local copies, waits for them, and re-layouts: 4.3 us -> 0.68 us
    select_n x0 -> x1, other arithmetic: none -> 2.41 us  [local(): return jnp.where(inside[:, None, :], visits - model[None], jnp.float32(0.0))]
    pallas_call x1, Pallas kernels: 26.3 us -> 25.6 us  [local(): pl.pallas_call(functools.partial(kernel, lax.axis_size('tile'), peers), i...]
    and x0 -> x1, other arithmetic: none -> 0.64 us  [local(): inside = (column >= box[:, 0:1]) & (column < box[:, 0:1] + box[:, 1:2])]
    slice x0 -> x1, local copies, waits for them, and re-layouts: none -> 0.58 us  [local(): inside = (column >= box[:, 0:1]) & (column < box[:, 0:1] + box[:, 1:2])]
where the time goes in v4:
time: 31.5 us; the launch traced here: 31.3 us
  Pallas kernels  25.6 us (81%)
  other arithmetic  3.04 us (10%)
  local copies, waits for them, and re-layouts  1.33 us (4%)
  between operations  1.31 us (4%)
    pallas_call x1, Pallas kernels, local(): pl.pallas_call(functools.partial(kernel, lax.axis_size('tile'), peers), i...  25.6 us
    select_n x1, other arithmetic, local(): return jnp.where(inside[:, None, :], visits - model[None], jnp.float32(0.0))  2.41 us
    unnamed x4, local copies, waits for them, and re-layouts  0.68 us
    and x1, other arithmetic, local(): inside = (column >= box[:, 0:1]) & (column < box[:, 0:1] + box[:, 1:2])  0.64 us

profile of v4, /device:TPU:0, one launch (start us, length us, event | category | flops | bytes accessed | tf_op | source)
XLA Modules:
  0.0 31.3 jit_solution(16154079432810342963)
XLA Ops:
  0.0 0.0 copy-start
  0.0 0.0 copy-start.1
  0.0 0.7 %copy-done = s32[4,2]{0,1:T(2,128)S(1)} copy-done((s32[4,2]{0,1:T(2,128)S(1)}, s32[4,2]{0,1:T(2,128)}, u32[]{:S(2)}) %copy-start) | copy-done | bytes 56
  0.7 0.1 constant_dynamic-slice_fusion
  0.8 0.6 %fusion.2 = (s32[1,1]{0,1:T(1,128)}, s32[1,1]{0,1:T(1,128)}) fusion(s32[1,2]{0,1:T(2,128)S(1)} %constant_dynamic-slice_fusion), kind=kLoop, calls=%fused_computation.6 | loop fusion | bytes 16 | tf_op jit(solution)/shard_map/slice | solution.py:269
  2.6 0.6 %fusion.1 = pred[2048]{0:T(1024)(128)(4,1)S(1)} fusion(s32[]{:T(128)} %bitcast.1, s32[]{:T(128)} %bitcast), kind=kLoop, calls=%fused_computation.4 | loop fusion | flops 6144 | bytes 2056 | tf_op jit(solution)/shard_map/and | solution.py:269
  3.3 25.6 %shard_map.64 = f32[128,2048]{1,0:T(8,128)} custom-call(f32[16,21]{1,0:T(8,128)} %row_hbm.1, f32[16,21]{1,0:T(8,128)} %col_hbm.1, f32[6,1,16]{2,1,0:T(1,128)} %bitcast.7, f32[128,512]{1,0:T(8,128)} %own_hbm.1), custom_call_target="tpu_custom_call" | custom-call | tf_op jit(solution)/shard_map/pallas_call | solution.py:246
  28.9 0.0 copy-done.1
  28.9 2.4 %fusion = f32[1,128,2048]{2,1,0:T(8,128)} fusion(f32[1,128,2048]{2,1,0:T(8,128)S(1)} %copy-done.1, f32[128,2048]{1,0:T(8,128)} %shard_map.64, pred[2048]{0:T(1024)(128)(4,1)S(1)} %fusion.1), kind=kLoop, calls=%fused_computation.1 | loop fusion | flops 524288 | bytes 3147776 | tf_op jit(solution)/shard_map/jit(_where)/select_n | solution.py:270
Async XLA Ops:
  0.0 0.7 %copy-start = (s32[4,2]{0,1:T(2,128)S(1)}, s32[4,2]{0,1:T(2,128)}, u32[]{:S(2)}) copy-start(s32[4,2]{0,1:T(2,128)} %param.11) | copy-start | bytes 100
  0.0 28.9 %copy-start.1 = (f32[1,128,2048]{2,1,0:T(8,128)S(1)}, f32[1,128,2048]{2,1,0:T(8,128)}, u32[]{:S(2)}) copy-start(f32[1,128,2048]{2,1,0:T(8,128)} %param.10) | copy-start | bytes 3145732
